TPU v7x, 32 devices: a whole 2x2x4 slice. The times are simulated.
32 devices in a mesh: row: 4 (over y, x), col: 8 (over z, core).
Axes of the slice: x: 2, y: 2, z: 4, core: 2. Of those that a mesh axis runs over, the one named last changes fastest.
Arguments:
- state: float32 [3072, 3072], P('col', 'row'), may hold values from -300 to 300
- noise: float32 [3072, 3072], P('col', 'row'), may hold values from -6 to 6
- mod_shift: float32 [3072], P('col'), may hold values from -3 to 3
- mod_scale: float32 [3072], P('col'), may hold values from -2.5 to 2.5
- mod_gate: float32 [3072], P('col'), may hold values from 0.3 to 3
- w_in: bfloat16 [3072, 12288], P('row', 'col'), may hold values from -0.109375 to 0.109375
- b_in: float32 [12288], P('col'), may hold values from -3 to 3
- w_out: bfloat16 [3072, 12288], P('col', 'row'), may hold values from -0.0546875 to 0.0546875
- b_out: float32 [3072], P('col'), may hold values from -2.5 to 2.5
Outputs:
- purified: float32 [3072, 3072], P('col', 'row')
- predicted: float32 [3072, 3072], P('col', 'row')
All inputs are finite; a program needn't handle non-finite values.
Results may differ from a plain program's by a relative error of at most 0.00049.
Values may be sent and summed in bfloat16 or wider, within the bound.
A program may use at most 128 MiB of HBM per device.

v0:
```python
import math
import jax
import jax.numpy as jnp
from jax import lax
from jax.sharding import PartitionSpec as P

D = 3072
beta_now = 2.09
step_width = 0.02
sigma_now = 0.322


def on_device(state, noise, mod_shift, mod_scale, mod_gate, w_in, b_in, w_out, b_out):
    w_in_all = lax.all_gather(w_in, "row", axis=0, tiled=True)
    w_out_all = lax.all_gather(w_out, "row", axis=1, tiled=True)
    col_sums, squares = lax.psum((jnp.sum(state, axis=0), jnp.sum(state * state, axis=0)), "col")
    center = col_sums / D
    spread = squares / D - center * center
    normed = (
        (state - center[None, :]) * lax.rsqrt(spread[None, :] + 1e-06) * (1.0 + mod_scale[:, None])
        + mod_shift[:, None]
    ).astype(jnp.bfloat16)
    normed_all = lax.all_gather(normed, "col", axis=0, tiled=True)
    pre_act = lax.dot_general(
        w_in_all, normed_all, (((0,), (0,)), ((), ())), preferred_element_type=jnp.float32
    )
    hidden = jax.nn.gelu(pre_act + b_in[:, None], approximate=True).astype(jnp.bfloat16)
    hidden_all = lax.all_gather(hidden, "col", axis=0, tiled=True)
    mixed_out = jnp.dot(w_out_all, hidden_all, preferred_element_type=jnp.float32)
    branch = mixed_out + b_out[:, None]
    predicted = state + mod_gate[:, None] * branch
    purified = (
        state * (1.0 + 0.5 * beta_now * step_width)
        - beta_now * step_width / sigma_now * predicted
        + math.sqrt(beta_now * step_width) * noise
    )
    return (purified, predicted)


def solution(mesh):
    in_specs = (
        P("col", "row"),
        P("col", "row"),
        P("col"),
        P("col"),
        P("col"),
        P("row", "col"),
        P("col"),
        P("col", "row"),
        P("col"),
    )
    out_specs = (P("col", "row"), P("col", "row"))
    return jax.shard_map(
        on_device, mesh=mesh, in_specs=in_specs, out_specs=out_specs, check_vma=False
    )
```

profile of v0, /device:TPU:0, one launch (start us, length us, event | category | flops | bytes accessed | tf_op | source)
XLA Modules:
  0.0 473.4 jit_solution(9994325539912814488)
XLA Ops:
  7.2 0.0 all-gather.5.cloned.1.call-start
  7.2 0.7 broadcast_add_fusion
  7.9 1.4 fusion.11
  9.3 18.3 %all-reduce = (f32[768]{0:T(1024)S(1)}, f32[768]{0:T(1024)S(1)}) all-reduce(f32[768]{0:T(1024)S(1)} %get-tuple-element.5, f32[768]{0:T(1024)S(1)} %get-tuple-element.4), channel_id=1, replica_groups=mesh['row'=4,'col'=8] {'col'}, use_global_device_ids=true, to_apply=%region_3.0 | all-reduce | flops 1536 | bytes 12288 | tf_op jit(solution)/shard_map/psum | solution.py:16
  27.7 2.3 add_convert_fusion
  29.9 0.0 all-gather.5.cloned.1.call-update
  30.0 0.0 copy-start.2
  30.0 0.0 all-gather.7.cloned.1.call-start
  30.0 0.7 all-gather.7.cloned.1.call-update
  30.7 0.0 all-gather.11.cloned.1.call-start
  30.8 0.7 all-gather.11.cloned.1.call-update
  31.5 0.0 all-gather.9.cloned.1.call-start
  31.5 48.5 %all-gather.5.cloned.1.call-done = bf16[3072,768]{1,0:T(8,128)(2,1)} async-done(((bf16[384,768]{1,0:T(8,128)(2,1)}), bf16[3072,768]{1,0:T(8,128)(2,1)}) %all-gather.5.cloned.1.call-update) | async-done | bytes 4718608 | tf_op jit(solution)/shard_map/all_gather | solution.py:23
  80.1 97.0 %all-gather.7.cloned.1.call-done = bf16[3072,1536]{1,0:T(8,128)(2,1)} async-done(((bf16[768,1536]{1,0:T(8,128)(2,1)}), bf16[3072,1536]{1,0:T(8,128)(2,1)}) %all-gather.7.cloned.1.call-update) | async-done | bytes 9437200 | tf_op jit(solution)/shard_map/all_gather | solution.py:14
  177.1 0.0 copy-done.2
  177.1 13.7 %fusion.7 = bf16[1536,768]{0,1:T(8,128)(2,1)} fusion(bf16[3072,768]{1,0:T(8,128)(2,1)} %all-gather.5.cloned.1.call-done, bf16[3072,1536]{1,0:T(8,128)(2,1)} %all-gather.7.cloned.1.call-done, f32[1536]{0:T(1024)S(1)} %copy-done.2), kind=kOutput, calls=%fused_computation.8 | convolution fusion | flops 7259553792 | bytes 16521216 | tf_op jit(solution)/shard_map/dot_general | solution.py:24
  190.7 0.0 copy-start
  190.7 0.0 copy-start.1
  190.7 0.0 all-gather.9.cloned.1.call-update
  190.8 1.3 copy-done
  192.1 0.0 copy-start.3
  192.1 0.0 copy-start.4
  192.1 0.4 copy.11
  192.5 0.0 copy-done.1
  192.5 0.4 copy.13
  192.9 82.4 %all-gather.11.cloned.1.call-done = bf16[384,12288]{1,0:T(8,128)(2,1)} async-done(((bf16[384,3072]{1,0:T(8,128)(2,1)}), bf16[384,12288]{1,0:T(8,128)(2,1)}) %all-gather.11.cloned.1.call-update) | async-done | bytes 9437200 | tf_op jit(solution)/shard_map/all_gather | solution.py:15
  275.3 169.8 %all-gather.9.cloned.1.call-done = bf16[12288,768]{0,1:T(8,128)(2,1)} async-done(((bf16[1536,768]{0,1:T(8,128)(2,1)}), bf16[12288,768]{0,1:T(8,128)(2,1)}) %all-gather.9.cloned.1.call-update) | async-done | bytes 18874384 | tf_op jit(solution)/shard_map/all_gather | solution.py:28
  445.1 0.0 copy-done.3
  445.1 0.0 copy-done.4
  445.1 17.8 %multiply_add_fusion = (f32[384,768]{0,1:T(8,128)}, f32[384,768]{0,1:T(8,128)S(1)}) fusion(f32[384,768]{0,1:T(8,128)S(1)} %copy.13, f32[384,768]{0,1:T(8,128)S(1)} %copy.11, f32[384]{0:T(512)S(1)} %copy-done.3, bf16[12288,768]{0,1:T(8,128)(2,1)} %all-gather.9.cloned.1.call-done, bf16[384,12288]{1,0:T(8,128)(2,1)} %all-gather.11.cloned.1.call-done, ...), kind=kOutput, calls=%fused_computation.13 | convolution fusion | flops 7250116608 | bytes 33033216 | tf_op jit(solution)/shard_map/dot_general | solution.py:29
  462.8 2.7 copy.14
  465.5 1.4 copy.15
  (1 shorter events, 0.0 us)
Async XLA Ops:
  7.2 72.9 %all-gather.5.cloned.1.call-start = ((), (), s32[]{:S(2)}) async-start(), calls=%async_computation | async-start | bytes 5308416 | tf_op jit(solution)/shard_map/all_gather | solution.py:23
  30.0 147.1 %copy-start.2 = (f32[1536]{0:T(1024)S(1)}, f32[1536]{0:T(1024)}, u32[]{:S(2)}) copy-start(f32[1536]{0:T(1024)} %param.15) | copy-start | bytes 18436
  30.0 147.1 %all-gather.7.cloned.1.call-start = ((), (), s32[]{:S(2)}) async-start(), calls=%async_computation.1 | async-start | bytes 11796480 | tf_op jit(solution)/shard_map/all_gather | solution.py:14
  30.7 244.6 %all-gather.11.cloned.1.call-start = ((), (), s32[]{:S(2)}) async-start(), calls=%async_computation.3 | async-start | bytes 11796480 | tf_op jit(solution)/shard_map/all_gather | solution.py:15
  31.5 413.6 %all-gather.9.cloned.1.call-start = ((), (), s32[]{:S(2)}) async-start(), calls=%async_computation.2 | async-start | bytes 21233664 | tf_op jit(solution)/shard_map/all_gather | solution.py:28
  190.7 1.4 copy-start
  190.7 1.8 copy-start.1
  192.1 253.0 %copy-start.3 = (f32[384]{0:T(512)S(1)}, f32[384]{0:T(512)}, u32[]{:S(2)}) copy-start(f32[384]{0:T(512)} %param.17) | copy-start | bytes 4612
  192.1 253.0 %copy-start.4 = (f32[384]{0:T(512)S(1)}, f32[384]{0:T(512)}, u32[]{:S(2)}) copy-start(f32[384]{0:T(512)} %param.13) | copy-start | bytes 4612
Sparse Core Ops, SparseCore 0:
  30.1 49.9 all-gather.4
  81.9 95.1 all-gather.6
  178.9 96.3 all-gather.10
  276.8 168.2 all-gather.8
where the time goes:
time: 474 us; the launch traced here: 473 us
  waiting for transfers between devices  399 us (84%)
  matrix products  31.4 us (7%)
  blocking collectives  18.3 us (4%)
  between operations  13.8 us (3%)
  local copies, waits for them, and re-layouts  6.13 us (1%)
    all_gather x1, waiting for transfers between devices, on_device(): hidden_all = lax.all_gather(hidden, 'col', axis=0, tiled=True)  170 us
    all_gather x1, waiting for transfers between devices, on_device(): w_in_all = lax.all_gather(w_in, 'row', axis=0, tiled=True)  97 us
    all_gather x1, waiting for transfers between devices, on_device(): w_out_all = lax.all_gather(w_out, 'row', axis=1, tiled=True)  82.4 us
    all_gather x1, waiting for transfers between devices, on_device(): normed_all = lax.all_gather(normed, 'col', axis=0, tiled=True)  48.5 us
    psum x1, blocking collectives, on_device(): lax.psum((jnp.sum(state, axis=0), jnp.sum(state * state, axis=0)), 'col')  18.3 us
    dot_general x1, matrix products, on_device(): jnp.dot(w_out_all, hidden_all, preferred_element_type=jnp.float32)  17.8 us
    dot_general x1, matrix products, on_device(): lax.dot_general(w_in_all, normed_all, (((0,), (0,)), ((), ())), preferred...  13.7 us
  transfers between devices with their start and end apart: 4, of which 4 were waited for; matrix products, arithmetic and copies ran while one was open for 3% of the time, Pallas kernels for 0%

commit v1 on v0

--- a/solution.py
+++ b/solution.py
@@ -20,7 +20,12 @@
         (state - center[None, :]) * lax.rsqrt(spread[None, :] + 1e-06) * (1.0 + mod_scale[:, None])
         + mod_shift[:, None]
     ).astype(jnp.bfloat16)
-    normed_all = lax.all_gather(normed, "col", axis=0, tiled=True)
+    ring = [normed]
+    for hop in range(7):
+        ring.append(lax.ppermute(ring[-1], "col", [(dev, (dev + 1) % 8) for dev in range(8)]))
+    normed_all = jnp.roll(
+        jnp.concatenate(ring[::-1], axis=0), (lax.axis_index("col") + 1) * ring[0].shape[0], axis=0
+    )
     pre_act = lax.dot_general(
         w_in_all, normed_all, (((0,), (0,)), ((), ())), preferred_element_type=jnp.float32
     )

time: 474 us -> 406 us (0.86)
  waiting for transfers between devices: 399 us -> 315 us
  local copies, waits for them, and re-layouts: 6.13 us -> 24.1 us
    all_gather x1, waiting for transfers between devices: 97 us -> 0.01 us  [on_device(): w_in_all = lax.all_gather(w_in, 'row', axis=0, tiled=True)]
    ppermute x0 -> x7, waiting for transfers between devices: none -> 78.1 us  [on_device(): lax.ppermute(ring[-1], 'col', [(dev, (dev + 1) % 8) for dev in range(8)])]
    all_gather x1 -> x0, waiting for transfers between devices: 48.5 us -> none  [on_device(): normed_all = lax.all_gather(normed, 'col', axis=0, tiled=True)]
    unnamed x14 -> x34, local copies, waits for them, and re-layouts: 6.13 us -> 24.1 us
    all_gather x1, waiting for transfers between devices: 82.4 us -> 65.5 us  [on_device(): w_out_all = lax.all_gather(w_out, 'row', axis=1, tiled=True)]
  transfers between devices with their start and end apart: 4 -> 10, of which waited for: 4 -> 9; matrix products, arithmetic and copies ran while one was open for 3% -> 9% of each run, Pallas kernels for 0% -> 0%
where the time goes in v1:
time: 406 us; the launch traced here: 405 us
  waiting for transfers between devices  315 us (78%)
  matrix products  31.5 us (8%)
  local copies, waits for them, and re-layouts  24.1 us (6%)
  blocking collectives  18.3 us (5%)
  between operations  13.9 us (3%)
    all_gather x1, waiting for transfers between devices, on_device(): hidden_all = lax.all_gather(hidden, 'col', axis=0, tiled=True)  170 us
    ppermute x7, waiting for transfers between devices, on_device(): lax.ppermute(ring[-1], 'col', [(dev, (dev + 1) % 8) for dev in range(8)])  78.1 us
    all_gather x1, waiting for transfers between devices, on_device(): w_out_all = lax.all_gather(w_out, 'row', axis=1, tiled=True)  65.5 us
    unnamed x34, local copies, waits for them, and re-layouts  24.1 us
    psum x1, blocking collectives, on_device(): lax.psum((jnp.sum(state, axis=0), jnp.sum(state * state, axis=0)), 'col')  18.3 us
    dot_general x1, matrix products, on_device(): jnp.dot(w_out_all, hidden_all, preferred_element_type=jnp.float32)  17.8 us
    dot_general x1, matrix products, on_device(): lax.dot_general(w_in_all, normed_all, (((0,), (0,)), ((), ())), preferred...  13.7 us
  transfers between devices with their start and end apart: 10, of which 9 were waited for; matrix products, arithmetic and copies ran while one was open for 9% of the time, Pallas kernels for 0%

profile of v1, /device:TPU:0, one launch (start us, length us, event | category | flops | bytes accessed | tf_op | source)
XLA Modules:
  0.0 405.5 jit_solution(13741308397192889402)
XLA Ops:
  7.2 0.0 all-gather.4.cloned.1.call-start
  7.2 0.7 all-gather.4.cloned.1.call-update
  7.9 0.0 all-gather.8.cloned.1.call-start
  8.0 0.7 all-gather.8.cloned.1.call-update
  8.7 0.0 all-gather.6.cloned.1.call-start
  8.7 0.1 fusion.16
  8.9 18.3 %all-reduce = (f32[768]{0:T(1024)S(1)}, f32[768]{0:T(1024)S(1)}) all-reduce(f32[768]{0:T(1024)S(1)} %get-tuple-element.5, f32[768]{0:T(1024)S(1)} %get-tuple-element.4), channel_id=1, replica_groups=mesh['row'=4,'col'=8] {'col'}, use_global_device_ids=true, to_apply=%region_3.0 | all-reduce | flops 1536 | bytes 12288 | tf_op jit(solution)/shard_map/psum | solution.py:16
  27.3 0.2 add_convert_fusion
  27.5 0.1 collective-permute-start
  27.5 11.1 %collective-permute-done = bf16[384,768]{1,0:T(8,128)(2,1)S(1)} collective-permute-done((bf16[384,768]{1,0:T(8,128)(2,1)S(1)}, bf16[384,768]{1,0:T(8,128)(2,1)S(1)}, u32[]{:S(2)}, u32[]{:S(2)}) %collective-permute-start) | collective-permute-done | bytes 589856 | tf_op jit(solution)/shard_map/ppermute | solution.py:25
  38.6 0.0 collective-permute-start.1
  38.6 11.1 %collective-permute-done.1 = bf16[384,768]{1,0:T(8,128)(2,1)S(1)} collective-permute-done((bf16[384,768]{1,0:T(8,128)(2,1)S(1)}, bf16[384,768]{1,0:T(8,128)(2,1)S(1)}, u32[]{:S(2)}, u32[]{:S(2)}) %collective-permute-start.1) | collective-permute-done | bytes 589856 | tf_op jit(solution)/shard_map/ppermute | solution.py:25
  49.7 0.0 collective-permute-start.2
  49.7 11.1 %collective-permute-done.2 = bf16[384,768]{1,0:T(8,128)(2,1)S(1)} collective-permute-done((bf16[384,768]{1,0:T(8,128)(2,1)S(1)}, bf16[384,768]{1,0:T(8,128)(2,1)S(1)}, u32[]{:S(2)}, u32[]{:S(2)}) %collective-permute-start.2) | collective-permute-done | bytes 589856 | tf_op jit(solution)/shard_map/ppermute | solution.py:25
  60.8 0.0 collective-permute-start.3
  60.9 11.1 %collective-permute-done.3 = bf16[384,768]{1,0:T(8,128)(2,1)S(1)} collective-permute-done((bf16[384,768]{1,0:T(8,128)(2,1)S(1)}, bf16[384,768]{1,0:T(8,128)(2,1)S(1)}, u32[]{:S(2)}, u32[]{:S(2)}) %collective-permute-start.3) | collective-permute-done | bytes 589856 | tf_op jit(solution)/shard_map/ppermute | solution.py:25
  72.0 0.0 collective-permute-start.4
  72.0 11.1 %collective-permute-done.4 = bf16[384,768]{1,0:T(8,128)(2,1)S(1)} collective-permute-done((bf16[384,768]{1,0:T(8,128)(2,1)S(1)}, bf16[384,768]{1,0:T(8,128)(2,1)S(1)}, u32[]{:S(2)}, u32[]{:S(2)}) %collective-permute-start.4) | collective-permute-done | bytes 589856 | tf_op jit(solution)/shard_map/ppermute | solution.py:25
  83.1 0.8 copy-done.1
  83.9 11.2 %collective-permute-done.5 = bf16[384,768]{1,0:T(8,128)(2,1)} collective-permute-done((bf16[384,768]{1,0:T(8,128)(2,1)S(1)}, bf16[384,768]{1,0:T(8,128)(2,1)}, u32[]{:S(2)}, u32[]{:S(2)}) %collective-permute-start.5) | collective-permute-done | bytes 589856 | tf_op jit(solution)/shard_map/ppermute | solution.py:25
  95.1 0.0 collective-permute-start.6
  95.1 11.4 %collective-permute-done.6 = bf16[384,768]{1,0:T(8,128)(2,1)} collective-permute-done((bf16[384,768]{1,0:T(8,128)(2,1)}, bf16[384,768]{1,0:T(8,128)(2,1)}, u32[]{:S(2)}, u32[]{:S(2)}) %collective-permute-start.6) | collective-permute-done | bytes 589856 | tf_op jit(solution)/shard_map/ppermute | solution.py:25
  106.5 1.9 constant_dynamic-update-slice_fusion.15
  108.4 1.9 constant_dynamic-update-slice_fusion.14
  110.4 1.9 constant_dynamic-update-slice_fusion.13
  112.3 0.8 constant_dynamic-update-slice_fusion.12
  113.2 0.9 constant_dynamic-update-slice_fusion.11
  114.0 0.9 constant_dynamic-update-slice_fusion.10
  114.9 0.9 constant_dynamic-update-slice_fusion.9
  115.8 1.1 constant_dynamic-update-slice_fusion.8
  116.8 2.0 constant_dynamic-update-slice_fusion.7
  118.9 2.0 constant_dynamic-update-slice_fusion.6
  120.9 0.9 constant_dynamic-update-slice_fusion.5
  121.7 0.9 constant_dynamic-update-slice_fusion.4
  122.6 0.9 constant_dynamic-update-slice_fusion.3
  123.5 0.9 constant_dynamic-update-slice_fusion.2
  124.3 0.9 constant_dynamic-update-slice_fusion.1
  125.2 1.0 constant_dynamic-update-slice_fusion
  126.3 13.7 %fusion.7 = bf16[1536,768]{0,1:T(8,128)(2,1)} fusion(bf16[3072,1536]{1,0:T(8,128)(2,1)} %all-gather.4.cloned.1.call-done, bf16[6144,768]{1,0:T(8,128)(2,1)} %constant_dynamic-update-slice_fusion, s32[]{:T(128)S(6)} %select_n.14, f32[1536]{0:T(1024)} %param.15), kind=kOutput, calls=%fused_computation.8 | convolution fusion | flops 7259553792 | bytes 16523268 | tf_op jit(solution)/shard_map/dot_general | solution.py:29
  140.0 0.0 all-gather.6.cloned.1.call-update
  140.0 0.4 copy.11
  140.4 0.9 copy-done.3
  141.2 0.4 copy.13
  141.6 65.5 %all-gather.8.cloned.1.call-done = bf16[384,12288]{1,0:T(8,128)(2,1)} async-done(((bf16[384,3072]{1,0:T(8,128)(2,1)}), bf16[384,12288]{1,0:T(8,128)(2,1)}) %all-gather.8.cloned.1.call-update) | async-done | bytes 9437200 | tf_op jit(solution)/shard_map/all_gather | solution.py:15
  207.2 169.9 %all-gather.6.cloned.1.call-done = bf16[12288,768]{0,1:T(8,128)(2,1)} async-done(((bf16[1536,768]{0,1:T(8,128)(2,1)}), bf16[12288,768]{0,1:T(8,128)(2,1)}) %all-gather.6.cloned.1.call-update) | async-done | bytes 18874384 | tf_op jit(solution)/shard_map/all_gather | solution.py:33
  377.1 17.8 %multiply_add_fusion = (f32[384,768]{0,1:T(8,128)}, f32[384,768]{0,1:T(8,128)S(1)}) fusion(f32[384,768]{0,1:T(8,128)S(1)} %copy.13, f32[384,768]{0,1:T(8,128)S(1)} %copy.11, f32[384]{0:T(512)S(1)} %copy-done.6, bf16[12288,768]{0,1:T(8,128)(2,1)} %all-gather.6.cloned.1.call-done, bf16[384,12288]{1,0:T(8,128)(2,1)} %all-gather.8.cloned.1.call-done, ...), kind=kOutput, calls=%fused_computation.15 | convolution fusion | flops 7250116608 | bytes 33033216 | tf_op jit(solution)/shard_map/dot_general | solution.py:34
  394.9 2.7 copy.14
  397.6 1.4 copy.15
  (18 shorter events, 0.0 us)
Async XLA Ops:
  7.2 1.6 copy-start
  7.2 20.1 %copy-start.5 = (f32[384]{0:T(512)S(1)}, f32[384]{0:T(512)}, u32[]{:S(2)}) copy-start(f32[384]{0:T(512)} %param.12) | copy-start | bytes 4612
  7.2 20.1 %copy-start.4 = (f32[384]{0:T(512)S(1)}, f32[384]{0:T(512)}, u32[]{:S(2)}) copy-start(f32[384]{0:T(512)} %param.11) | copy-start | bytes 4612
  7.2 119.1 %all-gather.4.cloned.1.call-start = ((), (), s32[]{:S(2)}) async-start(), calls=%async_computation | async-start | bytes 11796480 | tf_op jit(solution)/shard_map/all_gather | solution.py:14
  7.9 199.2 %all-gather.8.cloned.1.call-start = ((), (), s32[]{:S(2)}) async-start(), calls=%async_computation.2 | async-start | bytes 11796480 | tf_op jit(solution)/shard_map/all_gather | solution.py:15
  8.7 368.4 %all-gather.6.cloned.1.call-start = ((), (), s32[]{:S(2)}) async-start(), calls=%async_computation.1 | async-start | bytes 21233664 | tf_op jit(solution)/shard_map/all_gather | solution.py:33
  27.5 11.2 %collective-permute-start = (bf16[384,768]{1,0:T(8,128)(2,1)S(1)}, bf16[384,768]{1,0:T(8,128)(2,1)S(1)}, u32[]{:S(2)}, u32[]{:S(2)}) collective-permute-start(bf16[384,768]{1,0:T(8,128)(2,1)S(1)} %add_convert_fusion), channel_id=1, source_target_pairs={{0,1},{1,2},{2,3},{3,4},{4,5},{5,6},{6,7},{7,0},{8,9},{9,10},{10,1... | collective-permute-start | bytes 1769480 | tf_op jit(solution)/shard_map/ppermute | solution.py:25
  38.6 11.1 %collective-permute-start.1 = (bf16[384,768]{1,0:T(8,128)(2,1)S(1)}, bf16[384,768]{1,0:T(8,128)(2,1)S(1)}, u32[]{:S(2)}, u32[]{:S(2)}) collective-permute-start(bf16[384,768]{1,0:T(8,128)(2,1)S(1)} %collective-permute-done), channel_id=1, source_target_pairs={{0,1},{1,2},{2,3},{3,4},{4,5},{5,6},{6,7},{7,0},{8,9},{9,10},{10,1... | collective-permute-start | bytes 1769480 | tf_op jit(solution)/shard_map/ppermute | solution.py:25
  49.7 11.1 %collective-permute-start.2 = (bf16[384,768]{1,0:T(8,128)(2,1)S(1)}, bf16[384,768]{1,0:T(8,128)(2,1)S(1)}, u32[]{:S(2)}, u32[]{:S(2)}) collective-permute-start(bf16[384,768]{1,0:T(8,128)(2,1)S(1)} %collective-permute-done.1), channel_id=1, source_target_pairs={{0,1},{1,2},{2,3},{3,4},{4,5},{5,6},{6,7},{7,0},{8,9},{9,10},{10,1... | collective-permute-start | bytes 1769480 | tf_op jit(solution)/shard_map/ppermute | solution.py:25
  60.8 11.1 %collective-permute-start.3 = (bf16[384,768]{1,0:T(8,128)(2,1)S(1)}, bf16[384,768]{1,0:T(8,128)(2,1)S(1)}, u32[]{:S(2)}, u32[]{:S(2)}) collective-permute-start(bf16[384,768]{1,0:T(8,128)(2,1)S(1)} %collective-permute-done.2), channel_id=1, source_target_pairs={{0,1},{1,2},{2,3},{3,4},{4,5},{5,6},{6,7},{7,0},{8,9},{9,10},{10,1... | collective-permute-start | bytes 1769480 | tf_op jit(solution)/shard_map/ppermute | solution.py:25
  72.0 11.1 %collective-permute-start.4 = (bf16[384,768]{1,0:T(8,128)(2,1)S(1)}, bf16[384,768]{1,0:T(8,128)(2,1)S(1)}, u32[]{:S(2)}, u32[]{:S(2)}) collective-permute-start(bf16[384,768]{1,0:T(8,128)(2,1)S(1)} %collective-permute-done.3), channel_id=1, source_target_pairs={{0,1},{1,2},{2,3},{3,4},{4,5},{5,6},{6,7},{7,0},{8,9},{9,10},{10,1... | collective-permute-start | bytes 1769480 | tf_op jit(solution)/shard_map/ppermute | solution.py:25
  83.1 0.8 copy-start.1
  83.9 11.2 %collective-permute-start.5 = (bf16[384,768]{1,0:T(8,128)(2,1)S(1)}, bf16[384,768]{1,0:T(8,128)(2,1)}, u32[]{:S(2)}, u32[]{:S(2)}) collective-permute-start(bf16[384,768]{1,0:T(8,128)(2,1)S(1)} %collective-permute-done.4), channel_id=1, source_target_pairs={{0,1},{1,2},{2,3},{3,4},{4,5},{5,6},{6,7},{7,0},{8,9},{9,10},{10,1... | collective-permute-start | bytes 1769480 | tf_op jit(solution)/shard_map/ppermute | solution.py:25
  95.1 11.4 %collective-permute-start.6 = (bf16[384,768]{1,0:T(8,128)(2,1)}, bf16[384,768]{1,0:T(8,128)(2,1)}, u32[]{:S(2)}, u32[]{:S(2)}) collective-permute-start(bf16[384,768]{1,0:T(8,128)(2,1)} %collective-permute-done.5), channel_id=1, source_target_pairs={{0,1},{1,2},{2,3},{3,4},{4,5},{5,6},{6,7},{7,0},{8,9},{9,10},{10,1... | collective-permute-start | bytes 1769480 | tf_op jit(solution)/shard_map/ppermute | solution.py:25
  112.3 8.6 %copy-start.2 = (bf16[384,768]{1,0:T(8,128)(2,1)S(1)}, bf16[384,768]{1,0:T(8,128)(2,1)}, u32[]{:S(2)}) copy-start(bf16[384,768]{1,0:T(8,128)(2,1)} %copy-done.1) | copy-start | bytes 1769476
  140.0 1.3 copy-start.3
  140.0 237.1 %copy-start.6 = (f32[384]{0:T(512)S(1)}, f32[384]{0:T(512)}, u32[]{:S(2)}) copy-start(f32[384]{0:T(512)} %param.17) | copy-start | bytes 4612
  140.0 237.1 %copy-start.7 = (f32[384]{0:T(512)S(1)}, f32[384]{0:T(512)}, u32[]{:S(2)}) copy-start(f32[384]{0:T(512)} %param.13) | copy-start | bytes 4612
Sparse Core Ops, SparseCore 0:
  9.9 99.0 all-gather.3
  110.8 96.3 all-gather.7
  208.8 168.2 all-gather.5
